TPU v7x, 32 devices: a whole 2x2x4 slice. The times are simulated.
32 devices in a mesh: groups: 2 (over x), view: 16 (over z, y, core).
Axes of the slice: x: 2, y: 2, z: 4, core: 2. Of those that a mesh axis runs over, the one named last changes fastest.
Arguments:
- query_vectors: bfloat16 [32, 16, 8, 4096], P(('groups', 'view')), parts along dimension 0, may hold values from -6 to 6
- key_vectors: bfloat16 [32, 16, 8, 4096], P(('groups', 'view')), parts along dimension 0, may hold values from -6 to 6
- value_vectors: bfloat16 [32, 16, 8, 4096], P(('groups', 'view')), parts along dimension 0, may hold values from -6 to 6
- request_of_slot: int32 [8], P('groups'), parts along dimension 0, may hold values from 0 to 2, as said below
Outputs:
- attended: bfloat16 [32, 16, 8, 4096], P(('groups', 'view')), parts along dimension 0
There are 2 independent parts, one for each index of `groups`. A program takes and returns all parts, laid end to end along the dimension named above; each array names one. Nothing has to cross between parts.
Inputs may be any that keep to these rules, and one draw needn't show every extreme that they name: `request_of_slot`: each request holds 1 to 2 slots, not necessarily consecutive, and one holds exactly 2.
All inputs are finite; a program needn't handle non-finite values.
Results may differ from a plain program's by a relative error of at most 0.0044.
Values may be sent and summed in bfloat16 or wider, within the bound.
A program may use at most 64 MiB of HBM per device.

v0:
```python
import jax
import jax.numpy as jnp
from jax import lax
from jax.sharding import PartitionSpec as P

HEADS = 32
HS = 128
ROWS = 16
COLS = 8


NEG_FILL = -1e30


def partner(value, axis, distance):
    return lax.ppermute(value, axis, [(i, i ^ 1 << distance) for i in range(lax.axis_size(axis))])


def masked_softmax(scores, allowed):
    scores = jnp.where(allowed, scores, NEG_FILL)
    maximum = jnp.max(scores, axis=-1)
    raised = jnp.exp(scores - maximum[..., None])
    totals = jnp.sum(raised, axis=-1)
    return (maximum, totals, raised.astype(jnp.bfloat16))


def combine(first_part, second_part):
    highest = jnp.maximum(first_part[0], second_part[0])
    first_scale = jnp.exp(first_part[0] - highest)
    second_scale = jnp.exp(second_part[0] - highest)
    denominator = first_part[1] * first_scale + second_part[1] * second_scale
    numerator = first_part[2] * first_scale[..., None] + second_part[2] * second_scale[..., None]
    return (numerator / denominator[..., None]).astype(jnp.bfloat16)


def into_rows(tensor, row_blocks, head_groups):
    trailing = tensor.shape[3:]
    block_rows = tensor.shape[0] // row_blocks
    width_cols = tensor.shape[1]
    group_heads = tensor.shape[2] // head_groups
    shaped = tensor.reshape(
        (row_blocks, block_rows, width_cols, head_groups, group_heads) + trailing
    )
    permuted = (0, 3, 1, 2, 4) + tuple(range(5, 5 + len(trailing)))
    return shaped.transpose(permuted).reshape(
        (row_blocks * head_groups, block_rows, width_cols, group_heads) + trailing
    )


def into_tokens(tensor, row_blocks, head_groups):
    trailing = tensor.shape[4:]
    block_rows = tensor.shape[1]
    width_cols = tensor.shape[2]
    group_heads = tensor.shape[3]
    shaped = tensor.reshape(
        (row_blocks, head_groups, block_rows, width_cols, group_heads) + trailing
    )
    permuted = (0, 2, 3, 1, 4) + tuple(range(5, 5 + len(trailing)))
    return shaped.transpose(permuted).reshape(
        (row_blocks * block_rows * width_cols, head_groups * group_heads) + trailing
    )


def shards(query_vectors, key_vectors, value_vectors, request_of_slot):
    scaling = HS ** (-0.5)
    token_count = ROWS * COLS
    partner_key, partner_value = partner((key_vectors, value_vectors), "view", 0)
    head_blocks = 4
    block_heads = HEADS // head_blocks
    own_query = query_vectors.reshape(token_count, head_blocks, block_heads, HS)
    both_keys = jnp.concatenate(
        [
            key_vectors.reshape(token_count, head_blocks, block_heads, HS),
            partner_key.reshape(token_count, head_blocks, block_heads, HS),
        ],
        axis=0,
    )
    both_values = jnp.concatenate(
        [
            value_vectors.reshape(token_count, head_blocks, block_heads, HS),
            partner_value.reshape(token_count, head_blocks, block_heads, HS),
        ],
        axis=0,
    )
    query_row = jnp.arange(token_count) // COLS
    key_row = jnp.arange(2 * token_count) % token_count // COLS
    local_allowed = query_row[:, None] != key_row[None, :]

    def local_block(triple):
        block_scores = (
            jnp.einsum("nhx,khx->hnk", triple[0], triple[1], preferred_element_type=jnp.float32)
            * scaling
        )
        block_peak, block_total, block_weights = masked_softmax(block_scores, local_allowed[None])
        block_sum = jnp.einsum(
            "hnk,khx->nhx", block_weights, triple[2], preferred_element_type=jnp.float32
        )
        return (block_peak.T, block_total.T, block_sum)

    block_peaks, block_totals, block_sums = lax.map(
        local_block,
        (
            jnp.moveaxis(own_query, 1, 0),
            jnp.moveaxis(both_keys, 1, 0),
            jnp.moveaxis(both_values, 1, 0),
        ),
    )
    local_peak = jnp.moveaxis(block_peaks, 0, 1).reshape(token_count, HEADS)
    local_total = jnp.moveaxis(block_totals, 0, 1).reshape(token_count, HEADS)
    local_sum = jnp.moveaxis(block_sums, 0, 1).reshape(token_count, HEADS, HS)
    device_count = lax.axis_size("view")
    slot_count = device_count // 4
    pass_images = device_count // 2
    head_groups = 8
    row_blocks = device_count // head_groups
    block_rows = ROWS // row_blocks
    slot_request = jnp.broadcast_to(
        request_of_slot[:, None], (request_of_slot.shape[0], 2 * COLS)
    ).reshape(-1)
    row_allowed = slot_request[:, None] == slot_request[None, :]

    def arrange(tensor):
        shaped = tensor.reshape(slot_count, 2, 2, block_rows, COLS, HS).transpose(1, 3, 0, 2, 4, 5)
        return shaped.reshape(2 * block_rows, pass_images * COLS, HS)

    def restore(tensor):
        trailing = tensor.shape[2:]
        shaped = tensor.reshape((2, block_rows, slot_count, 2, COLS) + trailing)
        permuted = (2, 0, 3, 1, 4) + tuple(range(5, 5 + len(trailing)))
        return shaped.transpose(permuted).reshape((device_count, block_rows, COLS) + trailing)

    def one_head(triple):
        row_scores = (
            jnp.einsum(
                "bnx,bkx->bnk",
                arrange(triple[0]),
                arrange(triple[1]),
                preferred_element_type=jnp.float32,
            )
            * scaling
        )
        row_peak, row_total, row_weights = masked_softmax(row_scores, row_allowed[None])
        row_sum = jnp.einsum(
            "bnk,bkx->bnx", row_weights, arrange(triple[2]), preferred_element_type=jnp.float32
        )
        return (restore(row_peak), restore(row_total), restore(row_sum))

    query_rows = into_rows(query_vectors.reshape(ROWS, COLS, HEADS, HS), row_blocks, head_groups)
    key_rows = into_rows(key_vectors.reshape(ROWS, COLS, HEADS, HS), row_blocks, head_groups)
    value_rows = into_rows(value_vectors.reshape(ROWS, COLS, HEADS, HS), row_blocks, head_groups)
    by_head = (
        jnp.moveaxis(
            lax.all_to_all(query_rows, "view", split_axis=0, concat_axis=0, tiled=True), 3, 0
        ),
        jnp.moveaxis(
            lax.all_to_all(key_rows, "view", split_axis=0, concat_axis=0, tiled=True), 3, 0
        ),
        jnp.moveaxis(
            lax.all_to_all(value_rows, "view", split_axis=0, concat_axis=0, tiled=True), 3, 0
        ),
    )
    row_peaks, row_totals, row_sums = lax.map(one_head, by_head)
    peak_part = jnp.moveaxis(row_peaks, 0, 3)
    total_part = jnp.moveaxis(row_totals, 0, 3)
    sum_part = jnp.moveaxis(row_sums, 0, 3)
    row_peak = lax.all_to_all(peak_part, "view", split_axis=0, concat_axis=0, tiled=True)
    row_total = lax.all_to_all(total_part, "view", split_axis=0, concat_axis=0, tiled=True)
    row_sum = lax.all_to_all(sum_part, "view", split_axis=0, concat_axis=0, tiled=True)
    row_peak = into_tokens(row_peak, row_blocks, head_groups)
    row_total = into_tokens(row_total, row_blocks, head_groups)
    row_sum = into_tokens(row_sum, row_blocks, head_groups)
    attended = combine((local_peak, local_total, local_sum), (row_peak, row_total, row_sum))
    return attended.reshape(1, ROWS, COLS, HEADS * HS)


def solution(mesh):
    return jax.shard_map(
        shards,
        mesh=mesh,
        in_specs=(
            P(("groups", "view"), None, None, None),
            P(("groups", "view"), None, None, None),
            P(("groups", "view"), None, None, None),
            P("groups"),
        ),
        out_specs=P(("groups", "view"), None, None, None),
        check_vma=False,
    )
```

profile of v0, /device:TPU:13, one launch (start us, length us, event | category | flops | bytes accessed | tf_op | source)
XLA Modules:
  0.0 191.3 jit_solution(3276017524597650835)
XLA Ops:
  0.0 2.5 %copy.68 = bf16[2,8,8,8,4,128]{5,2,1,4,3,0:T(8,128)(2,1)} copy(bf16[2,8,8,8,4,128]{5,2,4,3,1,0:T(8,128)(2,1)} %bitcast.210) | data formatting | bytes 2097152 | tf_op jit(solution)/shard_map/reshape;reshape | solution.py:41
  2.5 6.6 %all-to-all-start = ((bf16[16,8,8,4,128]{4,2,1,3,0:T(8,128)(2,1)}), bf16[16,8,8,4,128]{4,2,1,3,0:T(8,128)(2,1)S(1)}, u32[]{:S(2)}, u32[]{:S(2)}) async-start(bf16[16,8,8,4,128]{4,2,1,3,0:T(8,128)(2,1)} %bitcast.9), calls=%async_computation | async-start | bytes 2097152 | tf_op jit(solution)/shard_map/all_to_all | solution.py:153
  9.1 2.5 %copy.69 = bf16[2,8,8,8,4,128]{5,2,1,4,3,0:T(8,128)(2,1)} copy(bf16[2,8,8,8,4,128]{5,2,4,3,1,0:T(8,128)(2,1)} %bitcast.11) | data formatting | bytes 2097152 | tf_op jit(solution)/shard_map/reshape;reshape | solution.py:41
  11.5 22.4 %all-to-all-done = bf16[16,8,8,4,128]{4,2,1,3,0:T(8,128)(2,1)S(1)} async-done(((bf16[16,8,8,4,128]{4,2,1,3,0:T(8,128)(2,1)}), bf16[16,8,8,4,128]{4,2,1,3,0:T(8,128)(2,1)S(1)}, u32[]{:S(2)}, u32[]{:S(2)}) %all-to-all-start) | async-done | bytes 1048608 | tf_op jit(solution)/shard_map/all_to_all | solution.py:153
  33.9 4.9 %all-to-all-start.1 = ((bf16[16,8,8,4,128]{4,2,1,3,0:T(8,128)(2,1)}), bf16[16,8,8,4,128]{4,2,1,3,0:T(8,128)(2,1)}, u32[]{:S(2)}, u32[]{:S(2)}) async-start(bf16[16,8,8,4,128]{4,2,1,3,0:T(8,128)(2,1)} %bitcast.13), calls=%async_computation.1 | async-start | bytes 2097152 | tf_op jit(solution)/shard_map/all_to_all | solution.py:156
  38.9 2.6 %copy.70 = bf16[2,8,8,8,4,128]{5,2,1,4,3,0:T(8,128)(2,1)} copy(bf16[2,8,8,8,4,128]{5,2,4,3,1,0:T(8,128)(2,1)} %bitcast.15) | data formatting | bytes 2097152 | tf_op jit(solution)/shard_map/reshape;reshape | solution.py:41
  41.5 22.4 %all-to-all-done.1 = bf16[16,8,8,4,128]{4,2,1,3,0:T(8,128)(2,1)} async-done(((bf16[16,8,8,4,128]{4,2,1,3,0:T(8,128)(2,1)}), bf16[16,8,8,4,128]{4,2,1,3,0:T(8,128)(2,1)}, u32[]{:S(2)}, u32[]{:S(2)}) %all-to-all-start.1) | async-done | bytes 1048608 | tf_op jit(solution)/shard_map/all_to_all | solution.py:156
  63.8 4.9 %all-to-all-start.2 = ((bf16[16,8,8,4,128]{4,2,1,3,0:T(8,128)(2,1)}), bf16[16,8,8,4,128]{4,2,1,3,0:T(8,128)(2,1)}, u32[]{:S(2)}, u32[]{:S(2)}) async-start(bf16[16,8,8,4,128]{4,2,1,3,0:T(8,128)(2,1)} %bitcast.17), calls=%async_computation.2 | async-start | bytes 2097152 | tf_op jit(solution)/shard_map/all_to_all | solution.py:159
  69.6 2.4 %copy.97 = bf16[16,8,32,128]{3,2,1,0:T(8,128)(2,1)} copy(bf16[16,8,32,128]{3,1,2,0:T(8,128)(2,1)} %bitcast.87) | data formatting | bytes 2097152
  72.0 2.4 %copy.99 = bf16[16,8,32,128]{3,2,1,0:T(8,128)(2,1)} copy(bf16[16,8,32,128]{3,1,2,0:T(8,128)(2,1)} %bitcast.97) | data formatting | bytes 2097152
  74.6 2.4 %copy.98 = bf16[16,8,32,128]{3,2,1,0:T(8,128)(2,1)} copy(bf16[16,8,32,128]{3,1,2,0:T(8,128)(2,1)} %bitcast.92) | data formatting | bytes 2097152
  77.0 2.4 %copy.100 = bf16[16,8,32,128]{3,2,1,0:T(8,128)(2,1)} copy(bf16[16,8,32,128]{3,1,2,0:T(8,128)(2,1)} %bitcast.102) | data formatting | bytes 2097152
  79.5 14.3 %all-to-all-done.2 = bf16[16,8,8,4,128]{4,2,1,3,0:T(8,128)(2,1)} async-done(((bf16[16,8,8,4,128]{4,2,1,3,0:T(8,128)(2,1)}), bf16[16,8,8,4,128]{4,2,1,3,0:T(8,128)(2,1)}, u32[]{:S(2)}, u32[]{:S(2)}) %all-to-all-start.2) | async-done | bytes 1048608 | tf_op jit(solution)/shard_map/all_to_all | solution.py:159
  93.8 15.7 %while.31 = (s32[]{:T(128)}, f32[4,16,8,8]{3,2,0,1:T(8,128)S(1)}, f32[4,16,8,8]{3,2,0,1:T(8,128)}, f32[4,16,8,8,128]{4,3,2,0,1:T(8,128)}, bf16[4,16,8,8,128]{4,3...) while((s32[]{:T(128)}, f32[4,16,8,8]{3,2,0,1:T(8,128)S(1)}, ...), condition=%wide.region_7.8_spmd.clone, body=%wide.region_4.7_spmd.clone.sunk | while | flops 34015232 | bytes 7598457 | solution.py:162
  93.9 1.1 constant_dynamic-slice_fusion.15
  95.8 0.6 constant_dynamic-update-slice_fusion.7
  96.9 0.8 constant_dynamic-update-slice_fusion.8
  97.8 1.1 constant_dynamic-slice_fusion.15
  99.7 0.6 constant_dynamic-update-slice_fusion.7
  100.8 0.8 constant_dynamic-update-slice_fusion.8
  101.7 1.1 constant_dynamic-slice_fusion.15
  103.7 0.6 constant_dynamic-update-slice_fusion.7
  104.7 0.9 constant_dynamic-update-slice_fusion.8
  105.6 1.1 constant_dynamic-slice_fusion.15
  107.6 0.6 constant_dynamic-update-slice_fusion.7
  108.7 0.8 constant_dynamic-update-slice_fusion.8
  109.5 1.1 bitcast_bitcast_fusion
  110.6 0.8 reshape.262
  111.3 4.9 %all-to-all-start.5 = ((f32[16,1,256]{2,1,0:T(1,128)}), f32[16,1,256]{2,1,0:T(1,128)S(1)}, u32[]{:S(2)}, u32[]{:S(2)}) async-start(f32[16,1,256]{2,1,0:T(1,128)} %reshape.262), calls=%async_computation.5 | async-start | bytes 32768 | tf_op jit(solution)/shard_map/all_to_all | solution.py:167
  116.3 0.8 reshape.260
  117.1 3.3 %all-to-all-done.5 = f32[16,1,256]{2,1,0:T(1,128)S(1)} async-done(((f32[16,1,256]{2,1,0:T(1,128)}), f32[16,1,256]{2,1,0:T(1,128)S(1)}, u32[]{:S(2)}, u32[]{:S(2)}) %all-to-all-start.5) | async-done | bytes 16416 | tf_op jit(solution)/shard_map/all_to_all | solution.py:167
  120.4 5.8 %all-to-all-start.3 = ((f32[16,1,256]{2,1,0:T(1,128)}), f32[16,1,256]{2,1,0:T(1,128)S(1)}, u32[]{:S(2)}, u32[]{:S(2)}) async-start(f32[16,1,256]{2,1,0:T(1,128)} %reshape.260), calls=%async_computation.3 | async-start | bytes 32768 | tf_op jit(solution)/shard_map/all_to_all | solution.py:166
  126.2 4.2 %maximum_bitcast_fusion = (bf16[4,256,8,128]{3,2,0,1:T(8,128)(2,1)}, bf16[4,256,8,128]{3,2,0,1:T(8,128)(2,1)}) fusion(bf16[128,4,8,128]{3,2,1,0:T(8,128)(2,1)} %bitcast.214, bf16[128,4,8,128]{3,2,1,0:T(8,128)(2,1)S(1)} %bitcast.212, bf16[128,4,8,128]{3,2,1,0:T(8,128)(2,1)} %bitcast.215, bf16[128,4,8,128]{3,2,1,0:T(8,128)(2,1)} %bitcast.213), kind=kLoop, calls=%fused_computation.33 | loop fusion | flops 2097152 | bytes 8388608 | tf_op jit(solution)/shard_map/transpose | solution.py:104
  130.4 6.6 %all-to-all-start.4 = ((f32[16,8,8,4,128]{4,2,1,3,0:T(8,128)}), f32[16,8,8,4,128]{4,2,1,3,0:T(8,128)}, u32[]{:S(2)}, u32[]{:S(2)}) async-start(f32[16,8,8,4,128]{4,2,1,3,0:T(8,128)} %bitcast.217), calls=%async_computation.4 | async-start | bytes 4194304 | tf_op jit(solution)/shard_map/all_to_all | solution.py:168
  137.0 18.6 %while.30 = (s32[]{:T(128)}, f32[4,128,8]{1,2,0:T(8,128)S(1)}, f32[4,128,8]{1,2,0:T(8,128)S(1)}, f32[4,128,8,128]{1,3,2,0:T(8,128)}, bf16[4,128,8,128]{3,2,0,1:T...) while((s32[]{:T(128)}, f32[4,128,8]{1,2,0:T(8,128)S(1)}, ...), condition=%wide.region_3.4_spmd.clone, body=%wide.region_0.3_spmd.clone.sunk | while | flops 136083456 | bytes 8750721 | solution.py:100
  137.0 1.1 constant_dynamic-slice_fusion.11
  139.0 1.1 constant_dynamic-slice_fusion.13
  140.4 1.2 fusion.43
  141.6 1.1 constant_dynamic-slice_fusion.11
  142.9 0.4 fusion.41
  143.7 1.1 constant_dynamic-slice_fusion.13
  145.1 1.2 fusion.43
  146.3 1.1 constant_dynamic-slice_fusion.11
  148.3 1.1 constant_dynamic-slice_fusion.13
  149.7 1.2 fusion.43
  150.9 1.1 constant_dynamic-slice_fusion.11
  152.2 0.4 fusion.41
  153.0 1.1 constant_dynamic-slice_fusion.13
  154.4 1.2 fusion.43
  155.6 2.4 %copy.67 = f32[128,4,8,128]{3,2,1,0:T(8,128)S(1)} copy(f32[128,4,8,128]{0,3,2,1:T(8,128)} %bitcast.216) | data formatting | bytes 4194304 | tf_op jit(solution)/shard_map/transpose | solution.py:110
  158.0 1.6 reshape.239
  159.5 0.5 broadcast.109
  160.0 0.7 reduce
  161.1 0.7 reduce.1
  162.2 0.6 div.43
  162.8 1.5 div.44
  164.5 0.6 mul.57
  165.1 1.5 mul.58
  166.7 0.6 mul.54
  167.3 1.5 mul.55
  168.9 15.7 %all-to-all-done.4 = f32[16,8,8,4,128]{4,2,1,3,0:T(8,128)} async-done(((f32[16,8,8,4,128]{4,2,1,3,0:T(8,128)}), f32[16,8,8,4,128]{4,2,1,3,0:T(8,128)}, u32[]{:S(2)}, u32[]{:S(2)}) %all-to-all-start.4) | async-done | bytes 2097184 | tf_op jit(solution)/shard_map/all_to_all | solution.py:168
  184.5 2.0 %copy.78 = f32[2,8,8,8,4,128]{5,2,4,3,1,0:T(8,128)S(1)} copy(f32[2,8,8,8,4,128]{5,2,1,4,3,0:T(8,128)} %bitcast.24) | data formatting | bytes 4194304 | tf_op jit(solution)/shard_map/transpose | solution.py:59
  186.8 0.6 copy-done.1
  187.4 3.9 %divide_convert_fusion = bf16[1,16,8,4096]{3,2,1,0:T(8,128)(2,1)} fusion(f32[1,16,8,4096]{3,2,1,0:T(8,128)S(1)} %copy-done.1, f32[1,16,8,4096]{3,2,1,0:T(8,128)S(1)} %bitcast.203, f32[1,16,8,4096]{3,2,1,0:T(8,128)} %mul.58, f32[1,16,8,4096]{3,2,1,0:T(8,128)S(1)} %copy-done, f32[1,16,8,4096]{3,2,1,0:T(8,128)} %mul.55), kind=kLoop, calls=%fused_computation.35 | loop fusion | flops 2621440 | bytes 11534336 | tf_op jit(solution)/shard_map/convert_element_type | solution.py:33
  (114 shorter events, 11.4 us)
Async XLA Ops:
  2.5 31.4 %all-to-all-start = ((bf16[16,8,8,4,128]{4,2,1,3,0:T(8,128)(2,1)}), bf16[16,8,8,4,128]{4,2,1,3,0:T(8,128)(2,1)S(1)}, u32[]{:S(2)}, u32[]{:S(2)}) async-start(bf16[16,8,8,4,128]{4,2,1,3,0:T(8,128)(2,1)} %bitcast.9), calls=%async_computation | async-start | bytes 2097152 | tf_op jit(solution)/shard_map/all_to_all | solution.py:153
  33.9 29.9 %all-to-all-start.1 = ((bf16[16,8,8,4,128]{4,2,1,3,0:T(8,128)(2,1)}), bf16[16,8,8,4,128]{4,2,1,3,0:T(8,128)(2,1)}, u32[]{:S(2)}, u32[]{:S(2)}) async-start(bf16[16,8,8,4,128]{4,2,1,3,0:T(8,128)(2,1)} %bitcast.13), calls=%async_computation.1 | async-start | bytes 2097152 | tf_op jit(solution)/shard_map/all_to_all | solution.py:156
  38.9 30.4 %copy-start.2 = (bf16[1,16,8,4096]{3,2,1,0:T(8,128)(2,1)S(1)}, bf16[1,16,8,4096]{3,2,1,0:T(8,128)(2,1)}, u32[]{:S(2)}) copy-start(bf16[1,16,8,4096]{3,2,1,0:T(8,128)(2,1)} %param.8) | copy-start | bytes 3145732
  63.8 29.9 %all-to-all-start.2 = ((bf16[16,8,8,4,128]{4,2,1,3,0:T(8,128)(2,1)}), bf16[16,8,8,4,128]{4,2,1,3,0:T(8,128)(2,1)}, u32[]{:S(2)}, u32[]{:S(2)}) async-start(bf16[16,8,8,4,128]{4,2,1,3,0:T(8,128)(2,1)} %bitcast.17), calls=%async_computation.2 | async-start | bytes 2097152 | tf_op jit(solution)/shard_map/all_to_all | solution.py:159
  68.8 5.8 %collective-permute-start = (bf16[1,16,8,4096]{3,2,1,0:T(8,128)(2,1)}, bf16[1,16,8,4096]{3,2,1,0:T(8,128)(2,1)}, u32[]{:S(2)}, u32[]{:S(2)}) collective-permute-start(bf16[1,16,8,4096]{3,2,1,0:T(8,128)(2,1)} %param.9), channel_id=1, source_target_pairs={{0,1},{1,0},{2,3},{3,2},{4,5},{5,4},{6,7},{7,6},{8,9},{9,8},{10,11... | collective-permute-start | bytes 3145736 | tf_op jit(solution)/shard_map/ppermute | solution.py:16
  69.1 7.9 %collective-permute-start.1 = (bf16[1,16,8,4096]{3,2,1,0:T(8,128)(2,1)}, bf16[1,16,8,4096]{3,2,1,0:T(8,128)(2,1)}, u32[]{:S(2)}, u32[]{:S(2)}) collective-permute-start(bf16[1,16,8,4096]{3,2,1,0:T(8,128)(2,1)} %param.10), channel_id=1, source_target_pairs={{0,1},{1,0},{2,3},{3,2},{4,5},{5,4},{6,7},{7,6},{8,9},{9,8},{10,11... | collective-permute-start | bytes 3145736 | tf_op jit(solution)/shard_map/ppermute | solution.py:16
  69.6 4.9 %copy-start.4 = (s32[4]{0:T(128)S(1)}, s32[4]{0:T(128)}, u32[]{:S(2)}) copy-start(s32[4]{0:T(128)} %param.11) | copy-start | bytes 52
  109.5 16.7 %copy-start.3 = (bf16[16,8,32,128]{3,2,1,0:T(8,128)(2,1)S(1)}, bf16[16,8,32,128]{3,2,1,0:T(8,128)(2,1)}, u32[]{:S(2)}) copy-start(bf16[16,8,32,128]{3,2,1,0:T(8,128)(2,1)} %copy.97) | copy-start | bytes 3145732
  111.3 9.0 %all-to-all-start.5 = ((f32[16,1,256]{2,1,0:T(1,128)}), f32[16,1,256]{2,1,0:T(1,128)S(1)}, u32[]{:S(2)}, u32[]{:S(2)}) async-start(f32[16,1,256]{2,1,0:T(1,128)} %reshape.262), calls=%async_computation.5 | async-start | bytes 32768 | tf_op jit(solution)/shard_map/all_to_all | solution.py:167
  120.4 10.0 %all-to-all-start.3 = ((f32[16,1,256]{2,1,0:T(1,128)}), f32[16,1,256]{2,1,0:T(1,128)S(1)}, u32[]{:S(2)}, u32[]{:S(2)}) async-start(f32[16,1,256]{2,1,0:T(1,128)} %reshape.260), calls=%async_computation.3 | async-start | bytes 32768 | tf_op jit(solution)/shard_map/all_to_all | solution.py:166
  130.4 54.2 %all-to-all-start.4 = ((f32[16,8,8,4,128]{4,2,1,3,0:T(8,128)}), f32[16,8,8,4,128]{4,2,1,3,0:T(8,128)}, u32[]{:S(2)}, u32[]{:S(2)}) async-start(f32[16,8,8,4,128]{4,2,1,3,0:T(8,128)} %bitcast.217), calls=%async_computation.4 | async-start | bytes 4194304 | tf_op jit(solution)/shard_map/all_to_all | solution.py:168
  184.5 2.2 %copy-start = (f32[1,16,8,4096]{3,2,1,0:T(8,128)S(1)}, f32[1,16,8,4096]{3,2,1,0:T(8,128)}, u32[]{:S(2)}) copy-start(f32[1,16,8,4096]{3,2,1,0:T(8,128)} %reshape.239) | copy-start | bytes 6291460
  184.5 2.9 %copy-start.1 = (f32[1,16,8,4096]{3,2,1,0:T(8,128)S(1)}, f32[1,16,8,4096]{3,2,1,0:T(8,128)}, u32[]{:S(2)}) copy-start(f32[1,16,8,4096]{3,2,1,0:T(8,128)} %div.44) | copy-start | bytes 6291460
where the time goes:
time: 193 us; the launch traced here: 191 us
  waiting for transfers between devices  78.1 us (40%)
  local copies, waits for them, and re-layouts  57.5 us (30%)
  starting transfers between devices  34.3 us (18%)
  other arithmetic  12.1 us (6%)
  matrix products  8.63 us (4%)
    all_to_all x1, waiting for transfers between devices, shards(): lax.all_to_all(query_rows, 'view', split_axis=0, concat_axis=0, tiled=True)  22.4 us
    all_to_all x1, waiting for transfers between devices, shards(): lax.all_to_all(key_rows, 'view', split_axis=0, concat_axis=0, tiled=True)  22.4 us
    all_to_all x1, waiting for transfers between devices, shards(): lax.all_to_all(sum_part, 'view', split_axis=0, concat_axis=0, tiled=True)  15.7 us
    all_to_all x1, waiting for transfers between devices, shards(): lax.all_to_all(value_rows, 'view', split_axis=0, concat_axis=0, tiled=True)  14.3 us
    unnamed x21, local copies, waits for them, and re-layouts  13.7 us
    dynamic_slice x16, local copies, waits for them, and re-layouts, shards(): lax.map(local_block, (jnp.moveaxis(own_query, 1, 0), jnp.moveaxis(both_ke...  10.1 us
    another operation x3, local copies, waits for them, and re-layouts, into_rows(): tensor.reshape((row_blocks, block_rows, width_cols, head_groups, group_he...  7.58 us
    all_to_all x1, starting transfers between devices, shards(): lax.all_to_all(sum_part, 'view', split_axis=0, concat_axis=0, tiled=True)  6.63 us
  transfers between devices with their start and end apart: 8, of which 5 were waited for; matrix products, arithmetic and copies ran while one was open for 27% of the time, Pallas kernels for 0%

commit v1 on v0

--- a/solution.py
+++ b/solution.py
@@ -1,6 +1,8 @@
 import jax
 import jax.numpy as jnp
 from jax import lax
+from jax.experimental import pallas as pl
+from jax.experimental.pallas import tpu as pltpu
 from jax.sharding import PartitionSpec as P
 
 HEADS = 32
@@ -61,7 +63,7 @@
     )
 
 
-def shards(query_vectors, key_vectors, value_vectors, request_of_slot):
+def general_shards(query_vectors, key_vectors, value_vectors, request_of_slot):
     scaling = HS ** (-0.5)
     token_count = ROWS * COLS
     partner_key, partner_value = partner((key_vectors, value_vectors), "view", 0)
@@ -173,7 +175,241 @@
     return attended.reshape(1, ROWS, COLS, HEADS * HS)
 
 
+def pair_kernel(
+    req_ref, q_ref, k_ref, v_ref, o_ref,
+    queries, kv, outer, inner, crossing, ending, results, sums, peaks, totals,
+    swap_send, swap_recv, own_send, outer_recv, cross_send, inner_recv, end_send, out_send, out_recv,
+):
+    half, _, tokens, size = queries.shape
+    me = lax.axis_index("view")
+    domain = me % 2
+    slot = me // 4
+    other = 1 - domain
+    twin = me + other - domain
+    upper = slot // 2
+    end_slot = 3 * upper
+    mid_slot = 1 + upper
+    is_end = slot == end_slot
+    is_mid = slot == mid_slot
+    near = me + 4 * (end_slot + mid_slot - 2 * slot)
+    across = me + 4 * (3 - 2 * slot)
+
+    mine = req_ref[slot]
+    end_same = (req_ref[end_slot] == mine).astype(jnp.int32)
+    mid_same = (req_ref[mid_slot] == mine).astype(jnp.int32)
+    far_same = jnp.maximum(
+        (req_ref[3 - end_slot] == mine).astype(jnp.int32), (req_ref[3 - mid_slot] == mine).astype(jnp.int32)
+    )
+    near_same = jnp.minimum(end_same, mid_same)
+    paired = jnp.maximum(near_same, far_same)
+
+    def remote(src, dst, send, recv, device):
+        return pltpu.make_async_remote_copy(
+            src_ref=src, dst_ref=dst, send_sem=send, recv_sem=recv,
+            device_id={"view": device}, device_id_type=pl.DeviceIdType.MESH,
+        )
+
+    def lanes(at, group):
+        return pl.ds(pl.multiple_of((group * half + at) * size, size), size)
+
+    def swap(at, which):
+        source = (k_ref, v_ref, q_ref)[which].at[:, lanes(at, other)]
+        target = queries.at[at, domain] if which == 2 else kv.at[at, which, domain]
+        return remote(source, target, swap_send.at[which, at], swap_recv.at[which, at], twin)
+
+    def swapped(at, which):
+        source = (k_ref, v_ref, q_ref)[which].at[:, lanes(at, other)]
+        target = queries.at[at, other] if which == 2 else kv.at[at, which, other]
+        return remote(source, target, swap_send.at[which, at], swap_recv.at[which, at], twin)
+
+    def own_copy(at):
+        return remote(kv.at[at], outer.at[at], own_send.at[at], outer_recv.at[at], near)
+
+    def cross_copy(at):
+        return remote(crossing.at[at], inner.at[at], cross_send.at[at], inner_recv.at[at], across)
+
+    def end_copy(at):
+        return remote(ending.at[at], inner.at[at], end_send.at[at], inner_recv.at[at], near)
+
+    def out_copy(at):
+        return remote(
+            results.at[at], o_ref.at[:, lanes(at, domain)], out_send.at[at], out_recv.at[at], twin
+        )
+
+    barrier = pltpu.get_barrier_semaphore()
+    for device in (twin, near):
+        pl.semaphore_signal(barrier, inc=1, device_id={"view": device}, device_id_type=pl.DeviceIdType.MESH)
+
+    @pl.when(is_mid)
+    def _():
+        pl.semaphore_signal(barrier, inc=1, device_id={"view": across}, device_id_type=pl.DeviceIdType.MESH)
+        pl.semaphore_wait(barrier, 3)
+
+    @pl.when(is_end)
+    def _():
+        pl.semaphore_wait(barrier, 2)
+
+    @pl.loop(0, half)
+    def _(at):
+        swap(at, 0).start()
+        swap(at, 1).start()
+
+    @pl.loop(0, half)
+    def _(at):
+        swap(at, 2).start()
+
+    @pl.loop(0, half)
+    def _(at):
+        kv[at, 0, domain] = k_ref[:, lanes(at, domain)]
+        kv[at, 1, domain] = v_ref[:, lanes(at, domain)]
+        queries[at, domain] = q_ref[:, lanes(at, domain)]
+        swapped(at, 0).wait_recv()
+        swapped(at, 1).wait_recv()
+
+        @pl.when(is_end)
+        def _():
+            own_copy(at).start()
+
+    def pass_across(at):
+        @pl.when(is_mid)
+        def _():
+            own_copy(at).wait_recv()
+            crossing[at] = jnp.where(far_same > 0, kv[at], outer[at])
+            cross_copy(at).start()
+
+    def pass_out(at):
+        cross_copy(at).wait_recv()
+
+        @pl.when(is_mid)
+        def _():
+            ending[at] = jnp.where(near_same > 0, kv[at], inner[at])
+            end_copy(at).start()
+
+    scaling = size ** (-0.5)
+
+    def scores_of(at, keys):
+        return (
+            lax.dot_general(
+                queries[at].reshape(2 * tokens, size), keys, (((1,), (1,)), ((), ())),
+                preferred_element_type=jnp.float32,
+            )
+            * scaling
+        )
+
+    def own_part(at):
+        swapped(at, 2).wait_recv()
+        scores = scores_of(at, kv[at, 0].reshape(2 * tokens, size))
+        peak = jnp.max(scores, axis=1, keepdims=True)
+        raised = jnp.exp(scores - peak)
+        peaks[at] = peak
+        totals[at] = jnp.sum(raised, axis=1, keepdims=True)
+        sums[at] = jnp.dot(
+            raised.astype(jnp.bfloat16), kv[at, 1].reshape(2 * tokens, size), preferred_element_type=jnp.float32
+        )
+
+    def pair_part(at, keys, values):
+        scores = scores_of(at, keys.reshape(2 * tokens, size))
+        query_row = lax.broadcasted_iota(jnp.int32, scores.shape, 0) % tokens // COLS
+        key_row = lax.broadcasted_iota(jnp.int32, scores.shape, 1) % tokens // COLS
+        scores = jnp.where(query_row == key_row, scores, NEG_FILL)
+        scores = jnp.where(paired > 0, scores, NEG_FILL)
+        own_peak = peaks[at]
+        peak = jnp.maximum(own_peak, jnp.max(scores, axis=1, keepdims=True))
+        raised = jnp.exp(scores - peak)
+        kept = jnp.exp(own_peak - peak)
+        total = totals[at] * kept + jnp.sum(raised, axis=1, keepdims=True)
+        summed = sums[at] * kept + jnp.dot(
+            raised.astype(jnp.bfloat16), values.reshape(2 * tokens, size), preferred_element_type=jnp.float32
+        )
+        sums[at] = summed / total
+        o_ref[:, lanes(at, domain)] = sums[at, pl.ds(pl.multiple_of(domain * tokens, tokens), tokens)].astype(
+            jnp.bfloat16
+        )
+        results[at] = sums[at, pl.ds(pl.multiple_of(other * tokens, tokens), tokens)].astype(jnp.bfloat16)
+        out_copy(at).start()
+
+    def finish(at):
+        @pl.when(is_mid)
+        def _():
+            pair_part(
+                at,
+                jnp.where(near_same > 0, outer[at, 0], inner[at, 0]),
+                jnp.where(near_same > 0, outer[at, 1], inner[at, 1]),
+            )
+
+        @pl.when(is_end)
+        def _():
+            pair_part(at, inner[at, 0], inner[at, 1])
+
+    pass_across(0)
+    own_part(0)
+
+    @pl.loop(1, half)
+    def _(at):
+        pass_across(at)
+        pass_out(at - 1)
+        own_part(at)
+        finish(at - 1)
+
+    pass_out(half - 1)
+    finish(half - 1)
+
+    @pl.loop(0, half)
+    def _(at):
+        for which in range(3):
+            swap(at, which).wait_send()
+
+        @pl.when(is_end)
+        def _():
+            own_copy(at).wait_send()
+
+        @pl.when(is_mid)
+        def _():
+            cross_copy(at).wait_send()
+            end_copy(at).wait_send()
+
+        out_copy(at).wait_send()
+        remote(
+            results.at[at], o_ref.at[:, lanes(at, other)], out_send.at[at], out_recv.at[at], twin
+        ).wait_recv()
+
+
+def pair_shards(query_vectors, key_vectors, value_vectors, request_of_slot):
+    tokens = ROWS * COLS
+    half = HEADS // 2
+    flat = [tensor.reshape(tokens, HEADS * HS) for tensor in (query_vectors, key_vectors, value_vectors)]
+    vmem = pl.BlockSpec(memory_space=pltpu.VMEM)
+    bank = pltpu.VMEM((half, 2, 2, tokens, HS), jnp.bfloat16)
+    column = pltpu.VMEM((half, 2 * tokens, 1), jnp.float32)
+    each = pltpu.SemaphoreType.DMA((half,))
+    three = pltpu.SemaphoreType.DMA((3, half))
+    pair_flops = 2 * 2 * 2 * (2 * tokens) * (2 * tokens) * HS * half
+    out = pl.pallas_call(
+        pair_kernel,
+        out_shape=jax.ShapeDtypeStruct((tokens, HEADS * HS), jnp.bfloat16),
+        in_specs=[pl.BlockSpec(memory_space=pltpu.SMEM), vmem, vmem, vmem],
+        out_specs=vmem,
+        scratch_shapes=[
+            pltpu.VMEM((half, 2, tokens, HS), jnp.bfloat16),
+            bank, bank, bank, bank, bank,
+            pltpu.VMEM((half, tokens, HS), jnp.bfloat16),
+            pltpu.VMEM((half, 2 * tokens, HS), jnp.float32),
+            column, column,
+            three, three, each, each, each, each, each, each, each,
+        ],
+        compiler_params=pltpu.CompilerParams(
+            collective_id=0, has_side_effects=True, vmem_limit_bytes=48 * 1024 * 1024
+        ),
+        cost_estimate=pl.CostEstimate(
+            flops=pair_flops, bytes_accessed=4 * tokens * HEADS * HS * 2, transcendentals=8 * tokens * tokens * half
+        ),
+    )(request_of_slot, *flat)
+    return out.reshape(1, ROWS, COLS, HEADS * HS)
+
+
 def solution(mesh):
+    slot_count = mesh.shape["view"] // 4
+    shards = pair_shards if slot_count == 4 else general_shards
     return jax.shard_map(
         shards,
         mesh=mesh,

time: 193 us -> 69.7 us (0.36)
  the two profiles are of different devices: /device:TPU:13 before, /device:TPU:0 now
where the time goes in v1:
time: 69.7 us; the launch traced here: 69.5 us
  Pallas kernels  64.1 us (92%)
  local copies, waits for them, and re-layouts  5.3 us (8%)
    pallas_call x1, Pallas kernels, pair_shards(): pl.pallas_call(pair_kernel, out_shape=jax.ShapeDtypeStruct((tokens, HEADS...  64.1 us
    unnamed x9, local copies, waits for them, and re-layouts  5.3 us

profile of v1, /device:TPU:0, one launch (start us, length us, event | category | flops | bytes accessed | tf_op | source)
XLA Modules:
  0.0 69.5 jit_solution(4548227026051277239)
XLA Ops:
  0.0 0.0 copy-start.3
  0.0 0.7 copy-done.3
  0.7 0.0 copy-start
  0.7 1.2 %copy-done = bf16[1,16,8,4096]{3,2,1,0:T(8,128)(2,1)S(1)} copy-done((bf16[1,16,8,4096]{3,2,1,0:T(8,128)(2,1)S(1)}, bf16[1,16,8,4096]{3,2,1,0:T(8,128)(2,1)}, u32[]{:S(2)}) %copy-start) | copy-done | bytes 1048600
  1.9 0.0 copy-start.1
  1.9 1.2 %copy-done.1 = bf16[1,16,8,4096]{3,2,1,0:T(8,128)(2,1)S(1)} copy-done((bf16[1,16,8,4096]{3,2,1,0:T(8,128)(2,1)S(1)}, bf16[1,16,8,4096]{3,2,1,0:T(8,128)(2,1)}, u32[]{:S(2)}) %copy-start.1) | copy-done | bytes 1048600
  3.1 0.0 copy-start.2
  3.1 1.2 %copy-done.2 = bf16[1,16,8,4096]{3,2,1,0:T(8,128)(2,1)S(1)} copy-done((bf16[1,16,8,4096]{3,2,1,0:T(8,128)(2,1)S(1)}, bf16[1,16,8,4096]{3,2,1,0:T(8,128)(2,1)}, u32[]{:S(2)}) %copy-start.2) | copy-done | bytes 1048600
  4.3 64.1 %shard_map.46 = bf16[128,4096]{1,0:T(8,128)(2,1)S(1)} custom-call(s32[4]{0:T(128)S(1)} %copy-done.3, bf16[128,4096]{1,0:T(8,128)(2,1)S(1)} %bitcast.5, bf16[128,4096]{1,0:T(8,128)(2,1)S(1)} %bitcast.6, bf16[128,4096]{1,0:T(8,128)(2,1)S(1)} %bitcast.7), custom_call_target="tpu_custom_call" | custom-call | flops 1073741824 | bytes 4194304 | tf_op jit(solution)/shard_map/pallas_call | solution.py:387
  68.5 1.0 %copy.6 = bf16[1,16,8,4096]{3,2,1,0:T(8,128)(2,1)} copy(bf16[1,16,8,4096]{3,2,1,0:T(8,128)(2,1)S(1)} %bitcast.4) | data formatting | bytes 2097152
Async XLA Ops:
  0.0 0.7 copy-start.3
  0.7 1.2 %copy-start = (bf16[1,16,8,4096]{3,2,1,0:T(8,128)(2,1)S(1)}, bf16[1,16,8,4096]{3,2,1,0:T(8,128)(2,1)}, u32[]{:S(2)}) copy-start(bf16[1,16,8,4096]{3,2,1,0:T(8,128)(2,1)} %param.4) | copy-start | bytes 3145732
  1.9 1.2 %copy-start.1 = (bf16[1,16,8,4096]{3,2,1,0:T(8,128)(2,1)S(1)}, bf16[1,16,8,4096]{3,2,1,0:T(8,128)(2,1)}, u32[]{:S(2)}) copy-start(bf16[1,16,8,4096]{3,2,1,0:T(8,128)(2,1)} %param.5) | copy-start | bytes 3145732
  3.1 1.2 %copy-start.2 = (bf16[1,16,8,4096]{3,2,1,0:T(8,128)(2,1)S(1)}, bf16[1,16,8,4096]{3,2,1,0:T(8,128)(2,1)}, u32[]{:S(2)}) copy-start(bf16[1,16,8,4096]{3,2,1,0:T(8,128)(2,1)} %param.6) | copy-start | bytes 3145732

commit v2 on v1

--- a/solution.py
+++ b/solution.py
@@ -9,6 +9,8 @@
 HS = 128
 ROWS = 16
 COLS = 8
+LOG2E = 1.4426950408889634
+VMEM_LIMIT = 60 * 1024 * 1024
 
 
 NEG_FILL = -1e30
@@ -175,12 +177,18 @@
     return attended.reshape(1, ROWS, COLS, HEADS * HS)
 
 
+PARTS = 4
+SKEW = 2
+AHEAD = 2
+
+
 def pair_kernel(
     req_ref, q_ref, k_ref, v_ref, o_ref,
-    queries, kv, outer, inner, crossing, ending, results, sums, peaks, totals,
-    swap_send, swap_recv, own_send, outer_recv, cross_send, inner_recv, end_send, out_send, out_recv,
+    queries, kv, outer, inner, crossing, ending, chosen, bias, results, sums, peaks, totals,
+    load_sem, swap_send, swap_recv, own_send, outer_recv, cross_send, inner_recv, end_send, out_send, out_recv,
 ):
     half, _, tokens, size = queries.shape
+    span = 4 // PARTS
     me = lax.axis_index("view")
     domain = me % 2
     slot = me // 4
@@ -212,28 +220,45 @@
     def lanes(at, group):
         return pl.ds(pl.multiple_of((group * half + at) * size, size), size)
 
-    def swap(at, which):
-        source = (k_ref, v_ref, q_ref)[which].at[:, lanes(at, other)]
-        target = queries.at[at, domain] if which == 2 else kv.at[at, which, domain]
-        return remote(source, target, swap_send.at[which, at], swap_recv.at[which, at], twin)
-
-    def swapped(at, which):
-        source = (k_ref, v_ref, q_ref)[which].at[:, lanes(at, other)]
-        target = queries.at[at, other] if which == 2 else kv.at[at, which, other]
-        return remote(source, target, swap_send.at[which, at], swap_recv.at[which, at], twin)
-
-    def own_copy(at):
-        return remote(kv.at[at], outer.at[at], own_send.at[at], outer_recv.at[at], near)
-
-    def cross_copy(at):
-        return remote(crossing.at[at], inner.at[at], cross_send.at[at], inner_recv.at[at], across)
-
-    def end_copy(at):
-        return remote(ending.at[at], inner.at[at], end_send.at[at], inner_recv.at[at], near)
-
-    def out_copy(at):
+    def unit(ref, number):
+        return ref.at[pl.ds(number * span, span)]
+
+    def place(at, which, owner):
+        return queries.at[at, owner] if which == 2 else kv.at[at * 4 + which * 2 + owner]
+
+    sources = (k_ref, v_ref, q_ref)
+
+    def load(at, which):
+        return pltpu.make_async_copy(
+            sources[which].at[:, lanes(at, domain)], place(at, which, domain), load_sem.at[which, at]
+        )
+
+    def swap(at, which, owner):
         return remote(
-            results.at[at], o_ref.at[:, lanes(at, domain)], out_send.at[at], out_recv.at[at], twin
+            sources[which].at[:, lanes(at, other)], place(at, which, owner),
+            swap_send.at[which, at], swap_recv.at[which, at], twin,
+        )
+
+    def fetch(at, which):
+        swap(at, which, domain).start()
+        load(at, which).start()
+
+    def fetched(at, which):
+        swap(at, which, other).wait_recv()
+        load(at, which).wait()
+
+    def own_copy(n):
+        return remote(unit(kv, n), unit(outer, n), own_send.at[n], outer_recv.at[n], near)
+
+    def cross_copy(n):
+        return remote(unit(crossing, n), unit(inner, n), cross_send.at[n], inner_recv.at[n], across)
+
+    def end_copy(n):
+        return remote(unit(ending, n), unit(inner, n), end_send.at[n], inner_recv.at[n], near)
+
+    def out_copy(at, group):
+        return remote(
+            results.at[at], o_ref.at[:, lanes(at, group)], out_send.at[at], out_recv.at[at], twin
         )
 
     barrier = pltpu.get_barrier_semaphore()
@@ -249,129 +274,147 @@
     def _():
         pl.semaphore_wait(barrier, 2)
 
-    @pl.loop(0, half)
-    def _(at):
-        swap(at, 0).start()
-        swap(at, 1).start()
-
-    @pl.loop(0, half)
-    def _(at):
-        swap(at, 2).start()
-
-    @pl.loop(0, half)
-    def _(at):
-        kv[at, 0, domain] = k_ref[:, lanes(at, domain)]
-        kv[at, 1, domain] = v_ref[:, lanes(at, domain)]
-        queries[at, domain] = q_ref[:, lanes(at, domain)]
-        swapped(at, 0).wait_recv()
-        swapped(at, 1).wait_recv()
-
-        @pl.when(is_end)
-        def _():
-            own_copy(at).start()
-
-    def pass_across(at):
+    for at in range(AHEAD):
+        for which in range(2):
+            fetch(at, which)
+
+    @pl.when(is_end)
+    def _():
+        @pl.loop(0, half)
+        def _(at):
+            @pl.when(at + AHEAD < half)
+            def _():
+                for which in range(2):
+                    fetch(at + AHEAD, which)
+
+            for which in range(2):
+                fetched(at, which)
+            for part in range(PARTS):
+                own_copy(at * PARTS + part).start()
+
+    for at in range(AHEAD):
+        fetch(at, 2)
+
+    query_row = lax.broadcasted_iota(jnp.int32, bias.shape, 0) % tokens // COLS
+    key_row = lax.broadcasted_iota(jnp.int32, bias.shape, 1) % tokens // COLS
+    bias[...] = jnp.where(paired > 0, jnp.where(query_row == key_row, 0.0, NEG_FILL), NEG_FILL)
+
+    def pass_across(n):
         @pl.when(is_mid)
         def _():
-            own_copy(at).wait_recv()
+            own_copy(n).wait_recv()
+            at = pl.ds(n * span, span)
             crossing[at] = jnp.where(far_same > 0, kv[at], outer[at])
-            cross_copy(at).start()
-
-    def pass_out(at):
-        cross_copy(at).wait_recv()
+            cross_copy(n).start()
+
+    def pass_out(n):
+        cross_copy(n).wait_recv()
 
         @pl.when(is_mid)
         def _():
+            at = pl.ds(n * span, span)
             ending[at] = jnp.where(near_same > 0, kv[at], inner[at])
-            end_copy(at).start()
-
-    scaling = size ** (-0.5)
+            end_copy(n).start()
+
+    scaling = size ** (-0.5) * LOG2E
 
     def scores_of(at, keys):
         return (
             lax.dot_general(
-                queries[at].reshape(2 * tokens, size), keys, (((1,), (1,)), ((), ())),
+                queries[at].reshape(2 * tokens, size), keys.reshape(2 * tokens, size), (((1,), (1,)), ((), ())),
                 preferred_element_type=jnp.float32,
             )
             * scaling
         )
 
+    def weighted(raised, values):
+        return jnp.dot(
+            raised.astype(jnp.bfloat16), values.reshape(2 * tokens, size), preferred_element_type=jnp.float32
+        )
+
     def own_part(at):
-        swapped(at, 2).wait_recv()
-        scores = scores_of(at, kv[at, 0].reshape(2 * tokens, size))
+        fetched(at, 2)
+        scores = scores_of(at, kv[pl.ds(at * 4, 2)])
         peak = jnp.max(scores, axis=1, keepdims=True)
-        raised = jnp.exp(scores - peak)
+        raised = jnp.exp2(scores - peak)
         peaks[at] = peak
         totals[at] = jnp.sum(raised, axis=1, keepdims=True)
-        sums[at] = jnp.dot(
-            raised.astype(jnp.bfloat16), kv[at, 1].reshape(2 * tokens, size), preferred_element_type=jnp.float32
-        )
-
-    def pair_part(at, keys, values):
-        scores = scores_of(at, keys.reshape(2 * tokens, size))
-        query_row = lax.broadcasted_iota(jnp.int32, scores.shape, 0) % tokens // COLS
-        key_row = lax.broadcasted_iota(jnp.int32, scores.shape, 1) % tokens // COLS
-        scores = jnp.where(query_row == key_row, scores, NEG_FILL)
-        scores = jnp.where(paired > 0, scores, NEG_FILL)
+        sums[at] = weighted(raised, kv[pl.ds(at * 4 + 2, 2)])
+
+    def finish(at):
+        @pl.when(is_mid)
+        def _():
+            chosen[...] = jnp.where(near_same > 0, outer[pl.ds(at * 4, 4)], inner[pl.ds(at * 4, 4)])
+
+        @pl.when(is_end)
+        def _():
+            chosen[...] = inner[pl.ds(at * 4, 4)]
+
+        scores = scores_of(at, chosen[pl.ds(0, 2)]) + bias[...]
         own_peak = peaks[at]
         peak = jnp.maximum(own_peak, jnp.max(scores, axis=1, keepdims=True))
-        raised = jnp.exp(scores - peak)
-        kept = jnp.exp(own_peak - peak)
+        raised = jnp.exp2(scores - peak)
+        kept = jnp.exp2(own_peak - peak)
         total = totals[at] * kept + jnp.sum(raised, axis=1, keepdims=True)
-        summed = sums[at] * kept + jnp.dot(
-            raised.astype(jnp.bfloat16), values.reshape(2 * tokens, size), preferred_element_type=jnp.float32
-        )
-        sums[at] = summed / total
+        sums[at] = (sums[at] * kept + weighted(raised, chosen[pl.ds(2, 2)])) / total
+        results[at] = sums[at, pl.ds(pl.multiple_of(other * tokens, tokens), tokens)].astype(jnp.bfloat16)
+        out_copy(at, domain).start()
         o_ref[:, lanes(at, domain)] = sums[at, pl.ds(pl.multiple_of(domain * tokens, tokens), tokens)].astype(
             jnp.bfloat16
         )
-        results[at] = sums[at, pl.ds(pl.multiple_of(other * tokens, tokens), tokens)].astype(jnp.bfloat16)
-        out_copy(at).start()
-
-    def finish(at):
+
+    def head(at, first):
         @pl.when(is_mid)
         def _():
-            pair_part(
-                at,
-                jnp.where(near_same > 0, outer[at, 0], inner[at, 0]),
-                jnp.where(near_same > 0, outer[at, 1], inner[at, 1]),
-            )
-
-        @pl.when(is_end)
-        def _():
-            pair_part(at, inner[at, 0], inner[at, 1])
-
-    pass_across(0)
-    own_part(0)
+            @pl.when(at + AHEAD < half)
+            def _():
+                for which in range(2):
+                    fetch(at + AHEAD, which)
+
+            for which in range(2):
+                fetched(at, which)
+
+        @pl.when(at + AHEAD < half)
+        def _():
+            fetch(at + AHEAD, 2)
+
+        for part in range(PARTS):
+            pass_across(at * PARTS + part)
+            if part >= SKEW or not first:
+                pass_out(at * PARTS + part - SKEW)
+            if part == 0:
+                own_part(at)
+            if part == PARTS // 2 and not first:
+                finish(at - 1)
+
+    head(0, True)
 
     @pl.loop(1, half)
     def _(at):
-        pass_across(at)
-        pass_out(at - 1)
-        own_part(at)
-        finish(at - 1)
-
-    pass_out(half - 1)
+        head(at, False)
+
+    for late in range(SKEW):
+        pass_out(half * PARTS - SKEW + late)
     finish(half - 1)
 
     @pl.loop(0, half)
     def _(at):
         for which in range(3):
-            swap(at, which).wait_send()
-
-        @pl.when(is_end)
-        def _():
-            own_copy(at).wait_send()
-
-        @pl.when(is_mid)
-        def _():
-            cross_copy(at).wait_send()
-            end_copy(at).wait_send()
-
-        out_copy(at).wait_send()
-        remote(
-            results.at[at], o_ref.at[:, lanes(at, other)], out_send.at[at], out_recv.at[at], twin
-        ).wait_recv()
+            swap(at, which, domain).wait_send()
+
+        for part in range(PARTS):
+
+            @pl.when(is_end)
+            def _():
+                own_copy(at * PARTS + part).wait_send()
+
+            @pl.when(is_mid)
+            def _():
+                cross_copy(at * PARTS + part).wait_send()
+                end_copy(at * PARTS + part).wait_send()
+
+        out_copy(at, domain).wait_send()
+        out_copy(at, other).wait_recv()
 
 
 def pair_shards(query_vectors, key_vectors, value_vectors, request_of_slot):
@@ -379,26 +422,30 @@
     half = HEADS // 2
     flat = [tensor.reshape(tokens, HEADS * HS) for tensor in (query_vectors, key_vectors, value_vectors)]
     vmem = pl.BlockSpec(memory_space=pltpu.VMEM)
-    bank = pltpu.VMEM((half, 2, 2, tokens, HS), jnp.bfloat16)
+    anywhere = pl.BlockSpec(memory_space=pl.ANY)
+    bank = pltpu.VMEM((half * 4, tokens, HS), jnp.bfloat16)
     column = pltpu.VMEM((half, 2 * tokens, 1), jnp.float32)
     each = pltpu.SemaphoreType.DMA((half,))
     three = pltpu.SemaphoreType.DMA((3, half))
+    units = pltpu.SemaphoreType.DMA((half * PARTS,))
     pair_flops = 2 * 2 * 2 * (2 * tokens) * (2 * tokens) * HS * half
     out = pl.pallas_call(
         pair_kernel,
         out_shape=jax.ShapeDtypeStruct((tokens, HEADS * HS), jnp.bfloat16),
-        in_specs=[pl.BlockSpec(memory_space=pltpu.SMEM), vmem, vmem, vmem],
+        in_specs=[pl.BlockSpec(memory_space=pltpu.SMEM), anywhere, anywhere, anywhere],
         out_specs=vmem,
         scratch_shapes=[
             pltpu.VMEM((half, 2, tokens, HS), jnp.bfloat16),
             bank, bank, bank, bank, bank,
+            pltpu.VMEM((4, tokens, HS), jnp.bfloat16),
+            pltpu.VMEM((2 * tokens, 2 * tokens), jnp.float32),
             pltpu.VMEM((half, tokens, HS), jnp.bfloat16),
             pltpu.VMEM((half, 2 * tokens, HS), jnp.float32),
             column, column,
-            three, three, each, each, each, each, each, each, each,
+            three, three, three, units, units, units, units, units, each, each,
         ],
         compiler_params=pltpu.CompilerParams(
-            collective_id=0, has_side_effects=True, vmem_limit_bytes=48 * 1024 * 1024
+            collective_id=0, has_side_effects=True, vmem_limit_bytes=VMEM_LIMIT
         ),
         cost_estimate=pl.CostEstimate(
             flops=pair_flops, bytes_accessed=4 * tokens * HEADS * HS * 2, transcendentals=8 * tokens * tokens * half

time: 69.7 us -> 93 us (1.33)
  Pallas kernels: 64.1 us -> 90.3 us
  local copies, waits for them, and re-layouts: 5.3 us -> 2.29 us
    pallas_call x1, Pallas kernels: 64.1 us -> 90.3 us  [pair_shards(): pl.pallas_call(pair_kernel, out_shape=jax.ShapeDtypeStruct((tokens, HEADS...]
    unnamed x9 -> x1, local copies, waits for them, and re-layouts: 5.3 us -> 2.29 us
where the time goes in v2:
time: 93 us; the launch traced here: 92.6 us
  Pallas kernels  90.3 us (97%)
  local copies, waits for them, and re-layouts  2.29 us (2%)
    pallas_call x1, Pallas kernels, pair_shards(): pl.pallas_call(pair_kernel, out_shape=jax.ShapeDtypeStruct((tokens, HEADS...  90.3 us
    unnamed x1, local copies, waits for them, and re-layouts  2.29 us

profile of v2, /device:TPU:0, one launch (start us, length us, event | category | flops | bytes accessed | tf_op | source)
XLA Modules:
  0.0 92.6 jit_solution(4702806102930784305)
XLA Ops:
  0.0 90.3 %shard_map.46 = bf16[128,4096]{1,0:T(8,128)(2,1)} custom-call(s32[4]{0:T(128)} %req_ref.1, bf16[128,4096]{1,0:T(8,128)(2,1)} %bitcast.5, bf16[128,4096]{1,0:T(8,128)(2,1)} %bitcast.6, bf16[128,4096]{1,0:T(8,128)(2,1)} %bitcast.7), custom_call_target="tpu_custom_call" | custom-call | flops 1073741824 | bytes 4194304 | tf_op jit(solution)/shard_map/pallas_call | solution.py:432
  90.3 2.3 %copy.6 = bf16[1,16,8,4096]{3,2,1,0:T(8,128)(2,1)} copy(bf16[1,16,8,4096]{3,2,1,0:T(8,128)(2,1)} %bitcast.4) | data formatting | bytes 2097152

commit v3 on v2

--- a/solution.py
+++ b/solution.py
@@ -10,7 +10,7 @@
 ROWS = 16
 COLS = 8
 LOG2E = 1.4426950408889634
-VMEM_LIMIT = 60 * 1024 * 1024
+VMEM_LIMIT = 209 * 256 * 1024
 
 
 NEG_FILL = -1e30
@@ -178,16 +178,18 @@
 
 
 PARTS = 4
-SKEW = 2
+SKEW = 4
+GROUPS = 2
 AHEAD = 2
 
 
 def pair_kernel(
-    req_ref, q_ref, k_ref, v_ref, o_ref,
-    queries, kv, outer, inner, crossing, ending, chosen, bias, results, sums, peaks, totals,
-    load_sem, swap_send, swap_recv, own_send, outer_recv, cross_send, inner_recv, end_send, out_send, out_recv,
+    req_hbm, q_ref, k_ref, v_ref, o_ref,
+    req_ref, queries, kv, outer, inner, crossing, ending, chosen, bias, results, sums, peaks, totals,
+    req_sem, load_sem, swap_send, swap_recv, own_send, outer_recv, cross_send, inner_recv, end_send, out_send, out_recv, out_sem,
 ):
-    half, _, tokens, size = queries.shape
+    half, _, _, rows, size = queries.shape
+    block = 2 * rows
     span = 4 // PARTS
     me = lax.axis_index("view")
     domain = me % 2
@@ -202,15 +204,6 @@
     near = me + 4 * (end_slot + mid_slot - 2 * slot)
     across = me + 4 * (3 - 2 * slot)
 
-    mine = req_ref[slot]
-    end_same = (req_ref[end_slot] == mine).astype(jnp.int32)
-    mid_same = (req_ref[mid_slot] == mine).astype(jnp.int32)
-    far_same = jnp.maximum(
-        (req_ref[3 - end_slot] == mine).astype(jnp.int32), (req_ref[3 - mid_slot] == mine).astype(jnp.int32)
-    )
-    near_same = jnp.minimum(end_same, mid_same)
-    paired = jnp.maximum(near_same, far_same)
-
     def remote(src, dst, send, recv, device):
         return pltpu.make_async_remote_copy(
             src_ref=src, dst_ref=dst, send_sem=send, recv_sem=recv,
@@ -224,18 +217,18 @@
         return ref.at[pl.ds(number * span, span)]
 
     def place(at, which, owner):
-        return queries.at[at, owner] if which == 2 else kv.at[at * 4 + which * 2 + owner]
+        return queries.at[at, :, owner] if which == 2 else kv.at[at * 4 + which * 2 + owner]
 
     sources = (k_ref, v_ref, q_ref)
 
     def load(at, which):
         return pltpu.make_async_copy(
-            sources[which].at[:, lanes(at, domain)], place(at, which, domain), load_sem.at[which, at]
+            sources[which].at[:, :, lanes(at, domain)], place(at, which, domain), load_sem.at[which, at]
         )
 
     def swap(at, which, owner):
         return remote(
-            sources[which].at[:, lanes(at, other)], place(at, which, owner),
+            sources[which].at[:, :, lanes(at, other)], place(at, which, owner),
             swap_send.at[which, at], swap_recv.at[which, at], twin,
         )
 
@@ -258,9 +251,14 @@
 
     def out_copy(at, group):
         return remote(
-            results.at[at], o_ref.at[:, lanes(at, group)], out_send.at[at], out_recv.at[at], twin
-        )
-
+            results.at[at, other], o_ref.at[:, :, lanes(at, group)], out_send.at[at], out_recv.at[at], twin
+        )
+
+    def keep_copy(at):
+        return pltpu.make_async_copy(results.at[at, domain], o_ref.at[:, :, lanes(at, domain)], out_sem.at[at])
+
+    request = pltpu.make_async_copy(req_hbm, req_ref, req_sem)
+    request.start()
     barrier = pltpu.get_barrier_semaphore()
     for device in (twin, near):
         pl.semaphore_signal(barrier, inc=1, device_id={"view": device}, device_id_type=pl.DeviceIdType.MESH)
@@ -295,8 +293,18 @@
     for at in range(AHEAD):
         fetch(at, 2)
 
-    query_row = lax.broadcasted_iota(jnp.int32, bias.shape, 0) % tokens // COLS
-    key_row = lax.broadcasted_iota(jnp.int32, bias.shape, 1) % tokens // COLS
+    request.wait()
+    mine = req_ref[slot]
+    end_same = (req_ref[end_slot] == mine).astype(jnp.int32)
+    mid_same = (req_ref[mid_slot] == mine).astype(jnp.int32)
+    far_same = jnp.maximum(
+        (req_ref[3 - end_slot] == mine).astype(jnp.int32), (req_ref[3 - mid_slot] == mine).astype(jnp.int32)
+    )
+    near_same = jnp.minimum(end_same, mid_same)
+    paired = jnp.maximum(near_same, far_same)
+
+    query_row = lax.broadcasted_iota(jnp.int32, bias.shape, 0) % rows // COLS
+    key_row = lax.broadcasted_iota(jnp.int32, bias.shape, 1) % rows // COLS
     bias[...] = jnp.where(paired > 0, jnp.where(query_row == key_row, 0.0, NEG_FILL), NEG_FILL)
 
     def pass_across(n):
@@ -318,28 +326,26 @@
 
     scaling = size ** (-0.5) * LOG2E
 
-    def scores_of(at, keys):
+    def scores_of(keys, asking):
         return (
-            lax.dot_general(
-                queries[at].reshape(2 * tokens, size), keys.reshape(2 * tokens, size), (((1,), (1,)), ((), ())),
-                preferred_element_type=jnp.float32,
-            )
-            * scaling
+            lax.dot_general(keys, asking, (((1,), (1,)), ((), ())), preferred_element_type=jnp.float32) * scaling
         )
 
     def weighted(raised, values):
-        return jnp.dot(
-            raised.astype(jnp.bfloat16), values.reshape(2 * tokens, size), preferred_element_type=jnp.float32
+        return lax.dot_general(
+            values, raised.astype(jnp.bfloat16), (((0,), (0,)), ((), ())), preferred_element_type=jnp.float32
         )
 
     def own_part(at):
         fetched(at, 2)
-        scores = scores_of(at, kv[pl.ds(at * 4, 2)])
-        peak = jnp.max(scores, axis=1, keepdims=True)
+        scores = scores_of(
+            kv[pl.ds(at * 4, 2)].reshape(GROUPS * block, size), queries[at].reshape(GROUPS * block, size)
+        )
+        peak = jnp.max(scores, axis=0, keepdims=True)
         raised = jnp.exp2(scores - peak)
         peaks[at] = peak
-        totals[at] = jnp.sum(raised, axis=1, keepdims=True)
-        sums[at] = weighted(raised, kv[pl.ds(at * 4 + 2, 2)])
+        totals[at] = jnp.sum(raised, axis=0, keepdims=True)
+        sums[at] = weighted(raised, kv[pl.ds(at * 4 + 2, 2)].reshape(GROUPS * block, size))
 
     def finish(at):
         @pl.when(is_mid)
@@ -350,18 +356,21 @@
         def _():
             chosen[...] = inner[pl.ds(at * 4, 4)]
 
-        scores = scores_of(at, chosen[pl.ds(0, 2)]) + bias[...]
-        own_peak = peaks[at]
-        peak = jnp.maximum(own_peak, jnp.max(scores, axis=1, keepdims=True))
-        raised = jnp.exp2(scores - peak)
-        kept = jnp.exp2(own_peak - peak)
-        total = totals[at] * kept + jnp.sum(raised, axis=1, keepdims=True)
-        sums[at] = (sums[at] * kept + weighted(raised, chosen[pl.ds(2, 2)])) / total
-        results[at] = sums[at, pl.ds(pl.multiple_of(other * tokens, tokens), tokens)].astype(jnp.bfloat16)
+        for group in range(GROUPS):
+            columns = slice(group * block, (group + 1) * block)
+            scores = scores_of(
+                chosen[0:2, group].reshape(block, size), queries[at, group].reshape(block, size)
+            ) + bias[...]
+            own_peak = peaks[at, :, columns]
+            peak = jnp.maximum(own_peak, jnp.max(scores, axis=0, keepdims=True))
+            raised = jnp.exp2(scores - peak)
+            kept = jnp.exp2(own_peak - peak)
+            total = totals[at, :, columns] * kept + jnp.sum(raised, axis=0, keepdims=True)
+            summed = sums[at, :, columns] * kept + weighted(raised, chosen[2:4, group].reshape(block, size))
+            attended = (summed / total).T.astype(jnp.bfloat16)
+            results[at, :, group] = attended.reshape(2, rows, size)
         out_copy(at, domain).start()
-        o_ref[:, lanes(at, domain)] = sums[at, pl.ds(pl.multiple_of(domain * tokens, tokens), tokens)].astype(
-            jnp.bfloat16
-        )
+        keep_copy(at).start()
 
     def head(at, first):
         @pl.when(is_mid)
@@ -382,9 +391,9 @@
             pass_across(at * PARTS + part)
             if part >= SKEW or not first:
                 pass_out(at * PARTS + part - SKEW)
-            if part == 0:
+            if part == 1:
                 own_part(at)
-            if part == PARTS // 2 and not first:
+            if part == PARTS - 1 and not first:
                 finish(at - 1)
 
     head(0, True)
@@ -413,42 +422,44 @@
                 cross_copy(at * PARTS + part).wait_send()
                 end_copy(at * PARTS + part).wait_send()
 
+        keep_copy(at).wait()
         out_copy(at, domain).wait_send()
         out_copy(at, other).wait_recv()
 
 
 def pair_shards(query_vectors, key_vectors, value_vectors, request_of_slot):
-    tokens = ROWS * COLS
+    rows = ROWS * COLS // GROUPS
     half = HEADS // 2
-    flat = [tensor.reshape(tokens, HEADS * HS) for tensor in (query_vectors, key_vectors, value_vectors)]
+    flat = [tensor.reshape(GROUPS, rows, HEADS * HS) for tensor in (query_vectors, key_vectors, value_vectors)]
     vmem = pl.BlockSpec(memory_space=pltpu.VMEM)
-    anywhere = pl.BlockSpec(memory_space=pl.ANY)
-    bank = pltpu.VMEM((half * 4, tokens, HS), jnp.bfloat16)
-    column = pltpu.VMEM((half, 2 * tokens, 1), jnp.float32)
+    hbm = pl.BlockSpec(memory_space=pltpu.HBM)
+    bank = pltpu.VMEM((half * 4, GROUPS, rows, HS), jnp.bfloat16)
+    line = pltpu.VMEM((half, 1, GROUPS * 2 * rows), jnp.float32)
     each = pltpu.SemaphoreType.DMA((half,))
     three = pltpu.SemaphoreType.DMA((3, half))
     units = pltpu.SemaphoreType.DMA((half * PARTS,))
-    pair_flops = 2 * 2 * 2 * (2 * tokens) * (2 * tokens) * HS * half
+    scores = (2 * ROWS * COLS) ** 2 * half
     out = pl.pallas_call(
         pair_kernel,
-        out_shape=jax.ShapeDtypeStruct((tokens, HEADS * HS), jnp.bfloat16),
-        in_specs=[pl.BlockSpec(memory_space=pltpu.SMEM), anywhere, anywhere, anywhere],
+        out_shape=jax.ShapeDtypeStruct((GROUPS, rows, HEADS * HS), jnp.bfloat16),
+        in_specs=[hbm, hbm, hbm, hbm],
         out_specs=vmem,
         scratch_shapes=[
-            pltpu.VMEM((half, 2, tokens, HS), jnp.bfloat16),
+            pltpu.SMEM(request_of_slot.shape, jnp.int32),
+            pltpu.VMEM((half, GROUPS, 2, rows, HS), jnp.bfloat16),
             bank, bank, bank, bank, bank,
-            pltpu.VMEM((4, tokens, HS), jnp.bfloat16),
-            pltpu.VMEM((2 * tokens, 2 * tokens), jnp.float32),
-            pltpu.VMEM((half, tokens, HS), jnp.bfloat16),
-            pltpu.VMEM((half, 2 * tokens, HS), jnp.float32),
-            column, column,
-            three, three, three, units, units, units, units, units, each, each,
+            pltpu.VMEM((4, GROUPS, rows, HS), jnp.bfloat16),
+            pltpu.VMEM((2 * rows, 2 * rows), jnp.float32),
+            pltpu.VMEM((half, 2, GROUPS, rows, HS), jnp.bfloat16),
+            pltpu.VMEM((half, HS, GROUPS * 2 * rows), jnp.float32),
+            line, line,
+            pltpu.SemaphoreType.DMA, three, three, three, units, units, units, units, units, each, each, each,
         ],
         compiler_params=pltpu.CompilerParams(
             collective_id=0, has_side_effects=True, vmem_limit_bytes=VMEM_LIMIT
         ),
         cost_estimate=pl.CostEstimate(
-            flops=pair_flops, bytes_accessed=4 * tokens * HEADS * HS * 2, transcendentals=8 * tokens * tokens * half
+            flops=6 * scores * HS, bytes_accessed=8 * ROWS * COLS * HEADS * HS, transcendentals=2 * scores
         ),
     )(request_of_slot, *flat)
     return out.reshape(1, ROWS, COLS, HEADS * HS)

time: 93 us -> 66.7 us (0.72)
  Pallas kernels: 90.3 us -> 64.6 us
    pallas_call x1, Pallas kernels: 90.3 us -> 64.6 us  [pair_shards(): pl.pallas_call(pair_kernel, out_shape=jax.ShapeDtypeStruct((GROUPS, rows,...]
    unnamed x1 -> x3, local copies, waits for them, and re-layouts: 2.29 us -> 1.63 us
where the time goes in v3:
time: 66.7 us; the launch traced here: 66.2 us
  Pallas kernels  64.6 us (97%)
  local copies, waits for them, and re-layouts  1.63 us (2%)
    pallas_call x1, Pallas kernels, pair_shards(): pl.pallas_call(pair_kernel, out_shape=jax.ShapeDtypeStruct((GROUPS, rows,...  64.6 us
    unnamed x3, local copies, waits for them, and re-layouts  1.63 us

profile of v3, /device:TPU:0, one launch (start us, length us, event | category | flops | bytes accessed | tf_op | source)
XLA Modules:
  0.0 66.2 jit_solution(14215618333505595219)
XLA Ops:
  0.0 0.0 copy-start
  0.0 0.7 copy-done
  0.7 64.6 %shard_map.46 = bf16[2,64,4096]{2,1,0:T(8,128)(2,1)S(1)} custom-call(s32[4]{0:T(128)S(1)} %copy-done, bf16[2,64,4096]{2,1,0:T(8,128)(2,1)} %bitcast.5, bf16[2,64,4096]{2,1,0:T(8,128)(2,1)} %bitcast.6, bf16[2,64,4096]{2,1,0:T(8,128)(2,1)} %bitcast.7), custom_call_target="tpu_custom_call" | custom-call | flops 805306368 | bytes 4194304 | tf_op jit(solution)/shard_map/pallas_call | solution.py:442
  65.2 1.0 %copy.6 = bf16[1,16,8,4096]{3,2,1,0:T(8,128)(2,1)} copy(bf16[1,16,8,4096]{3,2,1,0:T(8,128)(2,1)S(1)} %bitcast.4) | data formatting | bytes 2097152
Async XLA Ops:
  0.0 0.7 copy-start
